TPU v7x, 256 devices: a whole 4x4x8 slice. The times are simulated.
256 devices in a mesh: dp: 2 (over y_hi), mx: 16 (over x, y_lo, core), my: 8 (over z).
Axes of the slice: x: 4, y: 4 (y_hi: 2, y_lo: 2; y = y_hi * 2 + y_lo), z: 8, core: 2. Of those that a mesh axis runs over, the one named last changes fastest.
Arguments:
- normed_input: bfloat16 [2048, 6144], P('dp', 'mx'), may hold values from -6 to 6
- out_grad: bfloat16 [2048, 6144], P('dp', 'mx'), may hold values from -6 to 6
- w_in: bfloat16 [6144, 24576], P('mx', 'my'), may hold values from -0.078125 to 0.078125
- w_out: bfloat16 [24576, 6144], P('my', 'mx'), may hold values from -0.0390625 to 0.0390625
Outputs:
- in_grad: bfloat16 [2048, 6144], P(('dp', 'my'), 'mx')
- grad_w_in: bfloat16 [6144, 24576], P('mx', 'my')
- grad_w_out: bfloat16 [24576, 6144], P('my', 'mx')
All inputs are finite; a program needn't handle non-finite values.
Results may differ from a plain program's by a relative error of at most 0.03.
Values may be sent and summed in bfloat16 or wider, within the bound.
A program may use at most 128 MiB of HBM per device.

v0:
```python
import math

import jax
import jax.numpy as jnp
from jax import lax
from jax.sharding import PartitionSpec as P


def gelu_parts(pre):
    normal_cdf = 0.5 * (1.0 + lax.erf(pre * (1.0 / math.sqrt(2.0))))
    density = jnp.exp(-0.5 * pre * pre) * (1.0 / math.sqrt(2.0 * math.pi))
    return (pre * normal_cdf, normal_cdf + pre * density)


def contract(left, right, left_dim, right_dim):
    return lax.dot_general(
        left, right, (((left_dim,), (right_dim,)), ((), ())), preferred_element_type=jnp.float32
    )


def reduce_inputs(input_term):
    return lax.psum_scatter(
        input_term.astype(jnp.bfloat16), "my", scatter_dimension=0, tiled=True
    ).astype(jnp.float32)


def local(normed_input, out_grad, w_in, w_out):
    width = w_in.shape[1]
    pre_part = jnp.dot(normed_input, w_in, preferred_element_type=jnp.float32)
    grad_part = contract(out_grad, w_out, 1, 1)
    summed = lax.psum_scatter(
        jnp.concatenate([pre_part, grad_part], axis=1).astype(jnp.bfloat16),
        "mx",
        scatter_dimension=0,
        tiled=True,
    ).astype(jnp.float32)
    value, slope = gelu_parts(summed[:, :width])
    act = value.astype(jnp.bfloat16)
    pre_grad = (summed[:, width:] * slope).astype(jnp.bfloat16)
    act_full, pre_grad_full = (
        lax.all_gather(act, "mx", axis=0, tiled=True),
        lax.all_gather(pre_grad, "mx", axis=0, tiled=True),
    )
    part_out = contract(act_full, out_grad, 0, 0)
    part_in = contract(normed_input, pre_grad_full, 0, 0)
    input_term = contract(pre_grad_full, w_in, 1, 1)
    in_grad = reduce_inputs(input_term)
    grad_w_in, grad_w_out = (
        lax.psum(part_in.astype(jnp.bfloat16), "dp").astype(jnp.float32),
        lax.psum(part_out.astype(jnp.bfloat16), "dp").astype(jnp.float32),
    )
    return (
        in_grad.astype(jnp.bfloat16),
        grad_w_in.astype(jnp.bfloat16),
        grad_w_out.astype(jnp.bfloat16),
    )


def solution(mesh):
    in_specs = (P("dp", "mx"), P("dp", "mx"), P("mx", "my"), P("my", "mx"))
    out_specs = (P(("dp", "my"), "mx"), P("mx", "my"), P("my", "mx"))
    return jax.shard_map(local, mesh=mesh, in_specs=in_specs, out_specs=out_specs, check_vma=False)
```

profile of v0, /device:TPU:1, one launch (start us, length us, event | category | flops | bytes accessed | tf_op | source)
XLA Modules:
  0.0 452.8 jit_solution(9038777143271838931)
XLA Ops:
  7.2 0.0 copy-start
  7.2 0.0 copy-start.2
  7.2 0.0 reduce-scatter.3.cloned.1.call-start
  7.2 5.5 %convolution_convert_fusion = bf16[1024,3072]{1,0:T(8,128)(2,1)S(1)} fusion(bf16[1024,384]{1,0:T(8,128)(2,1)} %param.5, bf16[3072,384]{1,0:T(8,128)(2,1)} %param.7), kind=kOutput, calls=%fused_computation.1 | convolution fusion | flops 2419064832 | bytes 9437184 | tf_op jit(solution)/shard_map/dot_general | solution.py:16
  12.8 0.0 copy-done
  12.8 0.0 copy-done.2
  12.8 3.6 convolution_convert_fusion.1
  16.4 8.9 %pad_maximum_fusion = bf16[1024,6144]{1,0:T(8,128)(2,1)} fusion(bf16[1024,3072]{1,0:T(8,128)(2,1)S(1)} %convolution_convert_fusion, bf16[1024,3072]{1,0:T(8,128)(2,1)S(1)} %convolution_convert_fusion.1), kind=kLoop, calls=%fused_computation | loop fusion | flops 25165824 | bytes 25165824 | tf_op jit(solution)/shard_map/concatenate | solution.py:32
  25.4 0.0 copy-start.1
  25.4 0.0 reduce-scatter.3.cloned.1.call-update
  25.4 0.0 all-gather.5.cloned.1.call-start
  25.4 145.0 %reduce-scatter.3.cloned.1.call-done = bf16[64,6144]{1,0:T(8,128)(2,1)} async-done(((bf16[1024,6144]{1,0:T(8,128)(2,1)}), bf16[64,6144]{1,0:T(8,128)(2,1)}) %reduce-scatter.3.cloned.1.call-update) | async-done | bytes 786448 | tf_op jit(solution)/shard_map/reduce_scatter | solution.py:31
  170.4 1.2 convert_element_type.28
  171.7 1.3 multiply_convert_fusion
  172.9 0.0 all-gather.5.cloned.1.call-update
  172.9 0.0 all-gather.3.cloned.1.call-start
  173.0 0.7 all-gather.3.cloned.1.call-update
  173.7 0.2 all-reduce.3.cloned.1.call-start
  173.9 44.6 %all-gather.5.cloned.1.call-done = bf16[1024,3072]{1,0:T(8,128)(2,1)} async-done(((bf16[64,3072]{1,0:T(8,128)(2,1)}), bf16[1024,3072]{1,0:T(8,128)(2,1)}) %all-gather.5.cloned.1.call-update) | async-done | bytes 6291472 | tf_op jit(solution)/shard_map/all_gather | solution.py:41
  218.5 0.0 copy-done.1
  218.5 7.7 %convolution_convert_fusion.2 = bf16[3072,384]{1,0:T(8,128)(2,1)} fusion(bf16[1024,3072]{1,0:T(8,128)(2,1)} %all-gather.5.cloned.1.call-done, bf16[1024,384]{1,0:T(8,128)(2,1)S(1)} %copy-done.1), kind=kOutput, calls=%fused_computation.3 | convolution fusion | flops 2417098752 | bytes 9437184 | tf_op jit(solution)/shard_map/dot_general | solution.py:16
  226.2 39.9 %all-gather.3.cloned.1.call-done = bf16[1024,3072]{1,0:T(8,128)(2,1)} async-done(((bf16[64,3072]{1,0:T(8,128)(2,1)}), bf16[1024,3072]{1,0:T(8,128)(2,1)}) %all-gather.3.cloned.1.call-update) | async-done | bytes 6291472 | tf_op jit(solution)/shard_map/all_gather | solution.py:42
  266.1 7.8 %fusion = bf16[384,3072]{0,1:T(8,128)(2,1)} fusion(bf16[1024,3072]{1,0:T(8,128)(2,1)} %all-gather.3.cloned.1.call-done, bf16[1024,384]{1,0:T(8,128)(2,1)} %param.4), kind=kOutput, calls=%fused_computation.5 | convolution fusion | flops 2417098752 | bytes 9437184 | tf_op jit(solution)/shard_map/dot_general | solution.py:16
  273.9 0.0 all-reduce.3.cloned.1.call-update
  274.0 0.0 reduce-scatter.5.cloned.1.call-start
  274.0 6.5 %convolution_convert_fusion.4 = bf16[1024,384]{1,0:T(8,128)(2,1)} fusion(bf16[1024,3072]{1,0:T(8,128)(2,1)} %all-gather.3.cloned.1.call-done, bf16[384,3072]{1,0:T(8,128)(2,1)S(1)} %copy-done), kind=kOutput, calls=%fused_computation.6 | convolution fusion | flops 2416312320 | bytes 9437184 | tf_op jit(solution)/shard_map/dot_general | solution.py:16
  280.5 0.0 reduce-scatter.5.cloned.1.call-update
  280.5 126.9 %all-reduce.3.cloned.1.call-done = (bf16[384,3072]{0,1:T(8,128)(2,1)}, bf16[3072,384]{1,0:T(8,128)(2,1)}) async-done(((bf16[384,3072]{0,1:T(8,128)(2,1)}, bf16[3072,384]{1,0:T(8,128)(2,1)}), (bf16[384,3072]{0,1:T(8,128)(2,1)}, bf16[3072,384]{1,0:T(8,128)(2,1)})) %all-reduce.3.cloned.1.call-update) | async-done | bytes 4718608 | tf_op jit(solution)/shard_map/psum | solution.py:49
  407.4 4.3 copy.7
  411.6 31.4 %reduce-scatter.5.cloned.1.call-done = bf16[128,384]{1,0:T(8,128)(2,1)} async-done(((bf16[1024,384]{1,0:T(8,128)(2,1)}), bf16[128,384]{1,0:T(8,128)(2,1)}) %reduce-scatter.5.cloned.1.call-update) | async-done | bytes 98320 | tf_op jit(solution)/shard_map/reduce_scatter | solution.py:22
  443.0 3.3 copy.10
Async XLA Ops:
  7.2 5.6 %copy-start = (bf16[384,3072]{1,0:T(8,128)(2,1)S(1)}, bf16[384,3072]{1,0:T(8,128)(2,1)}, u32[]{:S(2)}) copy-start(bf16[384,3072]{1,0:T(8,128)(2,1)} %param.6) | copy-start | bytes 7077892
  7.2 5.6 %copy-start.2 = (bf16[1024,384]{1,0:T(8,128)(2,1)S(1)}, bf16[1024,384]{1,0:T(8,128)(2,1)}, u32[]{:S(2)}) copy-start(bf16[1024,384]{1,0:T(8,128)(2,1)} %param.4) | copy-start | bytes 2359300
  7.2 163.2 %reduce-scatter.3.cloned.1.call-start = ((), (), s32[]{:S(2)}) async-start(), calls=%async_computation.2 | async-start | bytes 13369344 | tf_op jit(solution)/shard_map/reduce_scatter | solution.py:31
  25.4 193.1 %copy-start.1 = (bf16[1024,384]{1,0:T(8,128)(2,1)S(1)}, bf16[1024,384]{1,0:T(8,128)(2,1)}, u32[]{:S(2)}) copy-start(bf16[1024,384]{1,0:T(8,128)(2,1)} %param.5) | copy-start | bytes 2359300
  25.4 193.1 %all-gather.5.cloned.1.call-start = ((), (), s32[]{:S(2)}) async-start(), calls=%async_computation.5 | async-start | bytes 6684672 | tf_op jit(solution)/shard_map/all_gather | solution.py:41
  172.9 93.2 %all-gather.3.cloned.1.call-start = ((), (), s32[]{:S(2)}) async-start(), calls=%async_computation.3 | async-start | bytes 6684672 | tf_op jit(solution)/shard_map/all_gather | solution.py:42
  173.7 233.7 %all-reduce.3.cloned.1.call-start = ((), (), s32[]{:S(2)}) async-start(), calls=%async_computation.6 | async-start | bytes 9437184 | tf_op jit(solution)/shard_map/psum | solution.py:49
  274.0 169.0 %reduce-scatter.5.cloned.1.call-start = ((), (), s32[]{:S(2)}) async-start(), calls=%async_computation.4 | async-start | bytes 884736 | tf_op jit(solution)/shard_map/reduce_scatter | solution.py:22
Sparse Core Ops, SparseCore 0:
  25.5 144.8 reduce-scatter.2
  173.1 45.3 all-gather.4
  220.4 45.6 all-gather.2
  274.1 133.2 all-reduce.2
  410.5 32.4 reduce-scatter.4
where the time goes:
time: 457 us; the launch traced here: 453 us
  waiting for transfers between devices  388 us (85%)
  matrix products  31.1 us (7%)
  between operations  13.8 us (3%)
  other arithmetic  11.4 us (2%)
  local copies, waits for them, and re-layouts  7.59 us (2%)
    reduce_scatter x1, waiting for transfers between devices, local(): lax.psum_scatter(jnp.concatenate([pre_part, grad_part], axis=1).astype(jn...  145 us
    psum x1, waiting for transfers between devices, local(): lax.psum(part_in.astype(jnp.bfloat16), 'dp').astype(jnp.float32)  127 us
    all_gather x1, waiting for transfers between devices, local(): lax.all_gather(act, 'mx', axis=0, tiled=True)  44.6 us
    all_gather x1, waiting for transfers between devices, local(): lax.all_gather(pre_grad, 'mx', axis=0, tiled=True)  39.9 us
    reduce_scatter x1, waiting for transfers between devices, reduce_inputs(): lax.psum_scatter(input_term.astype(jnp.bfloat16), 'my', scatter_dimension...  31.4 us
    dot_general x4, matrix products, contract(): lax.dot_general(left, right, (((left_dim,), (right_dim,)), ((), ())), pre...  27.5 us
  transfers between devices with their start and end apart: 5, of which 5 were waited for; matrix products, arithmetic and copies ran while one was open for 4% of the time, Pallas kernels for 0%

commit v1 on v0

v1 whole, which is shorter than its diff:
```python
import math

import jax
import jax.numpy as jnp
from jax import lax
from jax.experimental import pallas as pl
from jax.experimental.pallas import tpu as pltpu
from jax.sharding import PartitionSpec as P

MESH = pl.DeviceIdType.MESH
BF, F32 = jnp.bfloat16, jnp.float32

TOK = 1024
DC = 384
FH = 1536
SUB = 1
W = 128 * SUB
NC = FH // W
L1, L2, L3, L4, L5, L6, L7 = 1, 2, 3, 4, 5, 6, 7


def y_first(j):
    return lax.rem(j, 3) == 1


def gelu_parts(pre):
    normal_cdf = 0.5 * (1.0 + lax.erf(pre * (1.0 / math.sqrt(2.0))))
    density = jnp.exp(-0.5 * pre * pre) * (1.0 / math.sqrt(2.0 * math.pi))
    return (pre * normal_cdf, normal_cdf + pre * density)


def device(x, y, z, c):
    x, y, z = lax.rem(x + 4, 4), lax.rem(y + 4, 4), lax.rem(z + 8, 8)
    return (y // 2, x * 4 + lax.rem(y, 2) * 2 + c, z)


def position(x, y):
    x, y = lax.rem(x + 4, 4), lax.rem(y + 4, 4)
    return (y // 2) * 8 + x * 2 + lax.rem(y, 2)


def dot(a, b, ca=1, cb=0):
    return lax.dot_general(a, b, (((ca,), (cb,)), ((), ())), preferred_element_type=F32)


def wait(ref, sem):
    pltpu.make_async_copy(ref, ref, sem).wait()


def send(src, dst, ssem, rsem, to):
    pltpu.make_async_remote_copy(
        src_ref=src, dst_ref=dst, send_sem=ssem, recv_sem=rsem, device_id=to, device_id_type=MESH
    ).start()


def kernel(
    x_in, g_in, win_in, wout_in, ig_out, gwin_out, gwout_out,
    xc, xt, gc, win, wout, part, r_opp, r_left, r_right, fwd, y_buf, r_y, tile, s_in, s_out,
    ig_buf, ig_core, ig_z,
    load_sem, core_sem, core_send, w_load, w_core, w_send, rs_sem, rs_send, y_sem, y_send,
    a_sem, a_fwd, a_send, b_sem, b_fwd, b_send, dp_sem, dp_send, z_sem, z_send, xo_sem, xo_send,
    o_own, o_core, o_send, ic_sem, ic_send, iz_sem, iz_send,
):
    d, m, s = lax.axis_index("dp"), lax.axis_index("mx"), lax.axis_index("my")
    x, yl, c = m // 4, lax.rem(m // 2, 2), lax.rem(m, 2)
    y = d * 2 + yl
    core = device(x, y, s, 1 - c)
    right, left = device(x + 1, y, s, c), device(x + 3, y, s, c)
    pair = device(x, y + 1 - 2 * yl, s, c)
    across = device(x, y + 2, s, c)
    od = 1 - d
    mine = pl.ds(pl.multiple_of(c * DC, 128), DC)
    theirs = pl.ds(pl.multiple_of((1 - c) * DC, 128), DC)
    own_tok = pl.ds(pl.multiple_of(d * TOK, 128), TOK)
    other_tok = pl.ds(pl.multiple_of(od * TOK, 128), TOK)

    def hidden(core_of, j):
        return pl.ds(pl.multiple_of(core_of * FH + j * W, 128), W)

    def rows(j):
        return pl.ds(pl.multiple_of(j * W, 128), W)

    pltpu.make_async_copy(x_in, xc.at[:, mine], load_sem.at[0]).start()
    pltpu.make_async_copy(g_in, gc.at[own_tok, mine], load_sem.at[1]).start()

    @pl.loop(0, NC)
    def _(j):
        pltpu.make_async_copy(win_in.at[:, hidden(c, j)], win.at[j, mine], w_load.at[0, j]).start()
        pltpu.make_async_copy(wout_in.at[hidden(c, j)], wout.at[rows(j), mine], w_load.at[1, j]).start()

    peers = [device(x, y, s + k, c) for k in range(1, 8)]
    everyone = [core, right, left, device(x, y + 1, s, c), device(x, y + 3, s, c), across] + peers
    barrier = pltpu.get_barrier_semaphore()
    for peer in everyone:
        pl.semaphore_signal(barrier, inc=1, device_id=peer, device_id_type=MESH)
    pl.semaphore_wait(barrier, len(everyone))

    send(x_in, xc.at[:, mine], core_send.at[0], core_sem.at[0], core)
    send(g_in, gc.at[own_tok, mine], core_send.at[1], core_sem.at[1], core)

    @pl.loop(0, NC)
    def _(j):
        send(win_in.at[:, hidden(1 - c, j)], win.at[j, mine], w_send.at[0, j], w_core.at[0, j], core)
        send(wout_in.at[hidden(1 - c, j)], wout.at[rows(j), mine], w_send.at[1, j], w_core.at[1, j], core)

    wait(xc.at[:, mine], load_sem.at[0])
    wait(gc.at[own_tok, mine], load_sem.at[1])
    wait(xc.at[:, theirs], core_sem.at[0])
    wait(gc.at[own_tok, theirs], core_sem.at[1])

    nxt, prv, opp = lax.rem(x + 1, 4), lax.rem(x + 3, 4), lax.rem(x + 2, 4)

    def partial_sums(j):
        wait(win.at[j, mine], w_load.at[0, j])
        wait(wout.at[rows(j), mine], w_load.at[1, j])
        wait(win.at[j, theirs], w_core.at[0, j])
        wait(wout.at[rows(j), theirs], w_core.at[1, j])
        pre = dot(xc[...], win[j]).astype(BF)
        part[j, :, 0] = pre.reshape(8, 128, W)
        grad = dot(gc[own_tok, :], wout[rows(j), :], 1, 1).astype(BF)
        part[j, :, 1] = grad.reshape(8, 128, W)
        send(part.at[j, opp * 2], r_opp.at[j, 0], rs_send.at[0, j], rs_sem.at[0, j], right)
        send(part.at[j, opp * 2 + 1], r_opp.at[j, 1], rs_send.at[1, j], rs_sem.at[1, j], left)
        send(part.at[j, nxt * 2 + 1], r_left.at[j, 1], rs_send.at[2, j], rs_sem.at[2, j], right)
        send(part.at[j, prv * 2], r_right.at[j, 0], rs_send.at[3, j], rs_sem.at[3, j], left)

    def add_and_pass(j):
        wait(r_opp.at[j, 0], rs_sem.at[0, j])
        fwd[j, 0] = (part[j, nxt * 2].astype(F32) + r_opp[j, 0].astype(F32)).astype(BF)
        send(fwd.at[j, 0], r_left.at[j, 0], rs_send.at[4, j], rs_sem.at[4, j], right)
        wait(r_opp.at[j, 1], rs_sem.at[1, j])
        fwd[j, 1] = (part[j, prv * 2 + 1].astype(F32) + r_opp[j, 1].astype(F32)).astype(BF)
        send(fwd.at[j, 1], r_right.at[j, 1], rs_send.at[5, j], rs_sem.at[5, j], left)

    def x_sum(j, h):
        return part[j, x * 2 + h].astype(F32) + r_left[j, h].astype(F32) + r_right[j, h].astype(F32)

    def to_pair(j):
        wait(r_left.at[j, 1], rs_sem.at[2, j])
        wait(r_right.at[j, 0], rs_sem.at[3, j])
        wait(r_left.at[j, 0], rs_sem.at[4, j])
        wait(r_right.at[j, 1], rs_sem.at[5, j])
        y_buf[j] = x_sum(j, 1 - yl).astype(BF)
        send(y_buf.at[j], r_y.at[j], y_send.at[j], y_sem.at[j], pair)

    def ring(j):
        yf = y_first(j)

        def dev(da, db):
            return device(jnp.where(yf, x + db, x + da), jnp.where(yf, y + da, y + db), s, c)

        def pos(da, db):
            return position(jnp.where(yf, x + db, x + da), jnp.where(yf, y + da, y + db))

        return dev, pos

    def b_out(j, k, da):
        dev, pos = ring(j)
        ref = tile.at[j, pos(da, 0)]
        send(ref, ref, b_send.at[j], b_sem.at[0, j, k], dev(0, 1))
        send(ref, ref, b_send.at[j], b_sem.at[1, j, k], dev(0, 3))

    def activation(j):
        wait(r_y.at[j], y_sem.at[j])
        total = x_sum(j, yl) + r_y[j].astype(F32)
        value, slope = gelu_parts(total[0])
        pre_grad = (total[1] * slope).astype(BF)
        dev, pos = ring(j)
        for i in range(SUB):
            tile[j, pos(0, 0), 0, i] = value[:, i * 128 : (i + 1) * 128].T.astype(BF)
            tile[j, pos(0, 0), 1, i] = pre_grad[:, i * 128 : (i + 1) * 128]
        ref = tile.at[j, pos(0, 0)]
        send(ref, ref, a_send.at[j], a_sem.at[0, j], dev(1, 0))
        send(ref, ref, a_send.at[j], a_sem.at[1, j], dev(3, 0))
        b_out(j, 0, 0)

    def a_pass(j):
        dev, pos = ring(j)
        ref = tile.at[j, pos(3, 0)]
        wait(ref, a_sem.at[0, j])
        send(ref.at[0], ref.at[0], a_send.at[j], a_fwd.at[0, j], dev(1, 0))
        b_out(j, 1, 3)
        ref = tile.at[j, pos(1, 0)]
        wait(ref, a_sem.at[1, j])
        send(ref.at[1], ref.at[1], a_send.at[j], a_fwd.at[1, j], dev(3, 0))
        b_out(j, 2, 1)

    def a_last(j):
        dev, pos = ring(j)
        ref = tile.at[j, pos(2, 0)]
        wait(ref.at[0], a_fwd.at[0, j])
        wait(ref.at[1], a_fwd.at[1, j])
        b_out(j, 3, 2)

    order = (0, 3, 1, 2)

    def b_pass(j):
        dev, pos = ring(j)
        for k, da in enumerate(order):
            ref = tile.at[j, pos(da, 3)]
            wait(ref, b_sem.at[0, j, k])
            send(ref.at[0], ref.at[0], b_send.at[j], b_fwd.at[0, j, k], dev(0, 1))
            ref = tile.at[j, pos(da, 1)]
            wait(ref, b_sem.at[1, j, k])
            send(ref.at[1], ref.at[1], b_send.at[j], b_fwd.at[1, j, k], dev(0, 3))

    def weight_grads(j):
        dev, pos = ring(j)
        for k, da in enumerate(order):
            ref = tile.at[j, pos(da, 2)]
            wait(ref.at[0], b_fwd.at[0, j, k])
            wait(ref.at[1], b_fwd.at[1, j, k])
        for i in range(SUB):
            act = jnp.concatenate([tile[j, p, 0, i] for p in range(16)], axis=1)
            s_out[pl.ds(pl.multiple_of(j * W + i * 128, 128), 128), :] = dot(act, gc[...]).astype(BF)
        grads = [tile[j, :, 1, i].reshape(2 * TOK, 128) for i in range(SUB)]
        s_in[j] = dot(xt[...], jnp.concatenate(grads, axis=1) if SUB > 1 else grads[0]).astype(BF)
        to = gwin_out.at[:, hidden(c, j)]
        pltpu.make_async_copy(s_in.at[j, mine], to, o_own.at[0, j]).start()
        send(s_in.at[j, theirs], to, o_send.at[0, j], o_core.at[0, j], core)
        to = gwout_out.at[hidden(c, j)]
        pltpu.make_async_copy(s_out.at[rows(j), mine], to, o_own.at[1, j]).start()
        send(s_out.at[rows(j), theirs], to, o_send.at[1, j], o_core.at[1, j], core)

    def piece(of, z):
        tok = pl.ds(pl.multiple_of(of * TOK + z * 128, 128), 128)
        return xt.at[mine, tok], gc.at[tok, mine]

    def turn_inputs():
        xt[mine, own_tok] = xc[:, mine].T
        send(xt.at[mine, own_tok], xt.at[mine, own_tok], xo_send.at[0], xo_sem.at[0], core)
        for i, ref in enumerate(piece(d, s)):
            send(ref, ref, dp_send.at[i], dp_sem.at[i], across)

    def spread_inputs():
        for i, ref in enumerate(piece(od, s)):
            wait(ref, dp_sem.at[i])
            for k in range(7):
                send(ref, ref, z_send.at[i, k], z_sem.at[i, k], peers[k])

    def finish_inputs():
        for k in range(7):
            for i, ref in enumerate(piece(od, lax.rem(s + 7 - k, 8))):
                wait(ref, z_sem.at[i, k])
        send(xt.at[mine, other_tok], xt.at[mine, other_tok], xo_send.at[1], xo_sem.at[1], core)
        send(gc.at[other_tok, mine], gc.at[other_tok, mine], xo_send.at[2], xo_sem.at[2], core)

    def await_inputs():
        wait(xt.at[theirs, own_tok], xo_sem.at[0])
        wait(xt.at[theirs, other_tok], xo_sem.at[1])
        wait(gc.at[other_tok, theirs], xo_sem.at[2])

    def stage(t, lag, run):
        @pl.when((t >= lag) & (t < NC + lag))
        def _():
            run(t - lag)

    def at(t, when, run):
        pl.when(t == when)(run)

    @pl.loop(0, NC + L7)
    def _(t):
        stage(t, L1, add_and_pass)
        stage(t, L2, to_pair)
        stage(t, L3, activation)
        stage(t, 0, partial_sums)
        at(t, 0, turn_inputs)
        at(t, 2, spread_inputs)
        at(t, L7 - 1, finish_inputs)
        at(t, L7, await_inputs)
        stage(t, L4, a_pass)
        stage(t, L5, a_last)
        stage(t, L6, b_pass)
        stage(t, L7, weight_grads)

    total = None
    for j in range(NC):
        lhs = [tile[j, pl.ds(d * 8, 8), 1, i].reshape(TOK, 128) for i in range(SUB)]
        term = dot(jnp.concatenate(lhs, axis=1) if SUB > 1 else lhs[0], win[j], 1, 1)
        total = term if total is None else total + term
    total = total.astype(BF)
    ig_buf[0] = jnp.where(c == 0, total[:, :DC], total[:, DC:])
    ig_buf[1] = jnp.where(c == 0, total[:, DC:], total[:, :DC])
    send(ig_buf.at[1], ig_core, ic_send.at[0], ic_sem.at[0], core)
    wait(ig_core, ic_sem.at[0])
    ig_buf[0] = (ig_buf[0].astype(F32) + ig_core[...].astype(F32)).astype(BF)
    for k in range(7):
        to_z = lax.rem(s + k + 1, 8)
        tok = pl.ds(pl.multiple_of(to_z * 128, 128), 128)
        send(ig_buf.at[0, tok], ig_z.at[k], iz_send.at[k], iz_sem.at[k], peers[k])
    result = ig_buf[0, pl.ds(pl.multiple_of(s * 128, 128), 128), :].astype(F32)
    for k in range(7):
        wait(ig_z.at[k], iz_sem.at[k])
        result += ig_z[k].astype(F32)
    ig_out[...] = result.astype(BF)

    for i in range(2):
        wait(xc.at[:, mine], core_send.at[i])
        wait(piece(d, s)[i], dp_send.at[i])
        for k in range(7):
            wait(piece(od, s)[i], z_send.at[i, k])
    wait(xt.at[mine, own_tok], xo_send.at[0])
    wait(xt.at[mine, other_tok], xo_send.at[1])
    wait(gc.at[other_tok, mine], xo_send.at[2])
    wait(ig_buf.at[1], ic_send.at[0])
    for k in range(7):
        wait(ig_z.at[k], iz_send.at[k])

    @pl.loop(0, NC)
    def _(j):
        wait(win.at[j, mine], w_send.at[0, j])
        wait(wout.at[rows(j), mine], w_send.at[1, j])
        for i in range(6):
            wait(r_opp.at[j, 0], rs_send.at[i, j])
        wait(y_buf.at[j], y_send.at[j])
        wait(tile.at[j, pl.ds(0, 3)], a_send.at[j])
        wait(tile.at[j, pl.ds(0, 12)], b_send.at[j])
        wait(s_in.at[j, mine], o_own.at[0, j])
        wait(s_out.at[rows(j), mine], o_own.at[1, j])
        wait(s_in.at[j, theirs], o_send.at[0, j])
        wait(s_out.at[rows(j), theirs], o_send.at[1, j])
        wait(gwin_out.at[:, hidden(1 - c, j)], o_core.at[0, j])
        wait(gwout_out.at[hidden(1 - c, j)], o_core.at[1, j])


def local(normed_input, out_grad, w_in, w_out):
    any_space = pl.BlockSpec(memory_space=pl.ANY)
    dma = lambda *shape: pltpu.SemaphoreType.DMA(shape)
    vm = lambda *shape: pltpu.VMEM(shape, BF)
    return pl.pallas_call(
        kernel,
        out_shape=[
            jax.ShapeDtypeStruct((128, DC), BF),
            jax.ShapeDtypeStruct((DC, 2 * FH), BF),
            jax.ShapeDtypeStruct((2 * FH, DC), BF),
        ],
        in_specs=[any_space] * 4,
        out_specs=[pl.BlockSpec(memory_space=pltpu.VMEM), any_space, any_space],
        scratch_shapes=[
            vm(TOK, 2 * DC),
            vm(2 * DC, 2 * TOK),
            vm(2 * TOK, 2 * DC),
            vm(NC, 2 * DC, W),
            vm(FH, 2 * DC),
            vm(NC, 8, 2, 128, W),
            vm(NC, 2, 2, 128, W),
            vm(NC, 2, 2, 128, W),
            vm(NC, 2, 2, 128, W),
            vm(NC, 2, 2, 128, W),
            vm(NC, 2, 128, W),
            vm(NC, 2, 128, W),
            vm(NC, 16, 2, SUB, 128, 128),
            vm(NC, 2 * DC, W),
            vm(FH, 2 * DC),
            vm(2, TOK, DC),
            vm(TOK, DC),
            vm(7, 128, DC),
            dma(2), dma(2), dma(2),
            dma(2, NC), dma(2, NC), dma(2, NC),
            dma(6, NC), dma(6, NC), dma(NC), dma(NC),
            dma(2, NC), dma(2, NC), dma(NC),
            dma(2, NC, 4), dma(2, NC, 4), dma(NC),
            dma(2), dma(2), dma(2, 7), dma(2, 7), dma(3), dma(3),
            dma(2, NC), dma(2, NC), dma(2, NC),
            dma(1), dma(1), dma(7), dma(7),
        ],
        compiler_params=pltpu.CompilerParams(
            collective_id=0, has_side_effects=True, vmem_limit_bytes=62 << 20
        ),
        cost_estimate=pl.CostEstimate(flops=17 * 10**9, bytes_accessed=12 * 10**6, transcendentals=0),
    )(normed_input, out_grad, w_in, w_out)


def solution(mesh):
    in_specs = (P("dp", "mx"), P("dp", "mx"), P("mx", "my"), P("my", "mx"))
    out_specs = (P(("dp", "my"), "mx"), P("mx", "my"), P("my", "mx"))
    return jax.shard_map(local, mesh=mesh, in_specs=in_specs, out_specs=out_specs, check_vma=False)
```

time: 457 us -> 180 us (0.39)
  waiting for transfers between devices: 388 us -> 0 us
  Pallas kernels: 0 us -> 173 us
  matrix products: 31.1 us -> 0 us
  between operations: 13.8 us -> 0.64 us
  other arithmetic: 11.4 us -> 0 us
    reduce_scatter x2 -> x0, waiting for transfers between devices: 176 us -> none  [the longest x1 145 us: local(): lax.psum_scatter(jnp.concatenate([pre_part, grad_part], axis=1).astype(jn...]
    pallas_call x0 -> x1, Pallas kernels: none -> 173 us  [local(): pl.pallas_call(kernel, out_shape=[jax.ShapeDtypeStruct((128, DC), BF), ja...]
    psum x1 -> x0, waiting for transfers between devices: 127 us -> none  [local(): lax.psum(part_in.astype(jnp.bfloat16), 'dp').astype(jnp.float32)]
    all_gather x2 -> x0, waiting for transfers between devices: 84.5 us -> none  [the longest x1 44.6 us: local(): lax.all_gather(act, 'mx', axis=0, tiled=True)]
    dot_general x5 -> x0, matrix products: 31.1 us -> none  [the longest x4 27.5 us: contract(): lax.dot_general(left, right, (((left_dim,), (right_dim,)), ((), ())), pre...]
    concatenate x1 -> x0, other arithmetic: 8.95 us -> none  [local(): jnp.concatenate([pre_part, grad_part], axis=1).astype(jnp.bfloat16)]
  transfers between devices with their start and end apart: 5 -> 0, of which waited for: 5 -> 0; matrix products, arithmetic and copies ran while one was open for 4% -> 0% of each run, Pallas kernels for 0% -> 0%
where the time goes in v1:
time: 180 us
  Pallas kernels  173 us (96%)
  local copies, waits for them, and re-layouts  6.32 us (4%)
    pallas_call x1, Pallas kernels, local(): pl.pallas_call(kernel, out_shape=[jax.ShapeDtypeStruct((128, DC), BF), ja...  173 us
    unnamed x5, local copies, waits for them, and re-layouts  6.32 us

profile of v1, /device:TPU:1, one launch (start us, length us, event | category | flops | bytes accessed | tf_op | source)
XLA Modules:
  0.0 179.9 jit_solution(12404332657116776767)
XLA Ops:
  0.6 173.0 %shard_map.67 = (bf16[128,384]{1,0:T(8,128)(2,1)}, bf16[384,3072]{1,0:T(8,128)(2,1)}, bf16[3072,384]{1,0:T(8,128)(2,1)}) custom-call(bf16[1024,384]{1,0:T(8,128)(2,1)} %x_in.1, bf16[1024,384]{1,0:T(8,128)(2,1)} %g_in.1, bf16[384,3072]{1,0:T(8,128)(2,1)} %win_in.1, bf16[3072,384]{1,0:T(8,128)(2,1)} %wout_in.1), custom_call_target="tpu_custom_call" | custom-call | flops 16999999488 | bytes 12000000 | tf_op jit(solution)/shard_map/pallas_call | solution.py:330
  173.6 1.5 copy.10
  175.2 0.0 copy-start
  175.2 3.4 %copy.11 = bf16[384,3072]{1,0:T(8,128)(2,1)} copy(bf16[384,3072]{1,0:T(8,128)(2,1)} %get-tuple-element.7) | data formatting | bytes 4718592
  178.5 0.0 copy-done
  178.5 1.4 copy.12
Async XLA Ops:
  175.2 3.4 %copy-start = (bf16[3072,384]{1,0:T(8,128)(2,1)S(1)}, bf16[3072,384]{1,0:T(8,128)(2,1)}, u32[]{:S(2)}) copy-start(bf16[3072,384]{1,0:T(8,128)(2,1)} %get-tuple-element.8) | copy-start | bytes 7077892

commit v2 on v1

--- a/solution.py
+++ b/solution.py
@@ -13,14 +13,15 @@
 TOK = 1024
 DC = 384
 FH = 1536
-SUB = 1
+SUB = 2
 W = 128 * SUB
 NC = FH // W
 L1, L2, L3, L4, L5, L6, L7 = 1, 2, 3, 4, 5, 6, 7
+LAST = NC - 1
 
 
 def y_first(j):
-    return lax.rem(j, 3) == 1
+    return (j == 2) | (j == 3)
 
 
 def gelu_parts(pre):
@@ -56,7 +57,7 @@
 def kernel(
     x_in, g_in, win_in, wout_in, ig_out, gwin_out, gwout_out,
     xc, xt, gc, win, wout, part, r_opp, r_left, r_right, fwd, y_buf, r_y, tile, s_in, s_out,
-    ig_buf, ig_core, ig_z,
+    ig_acc, ig_buf, ig_core, ig_z,
     load_sem, core_sem, core_send, w_load, w_core, w_send, rs_sem, rs_send, y_sem, y_send,
     a_sem, a_fwd, a_send, b_sem, b_fwd, b_send, dp_sem, dp_send, z_sem, z_send, xo_sem, xo_send,
     o_own, o_core, o_send, ic_sem, ic_send, iz_sem, iz_send,
@@ -194,22 +195,43 @@
 
     order = (0, 3, 1, 2)
 
+    PARTS = ((slice(0, 2), None),) + ((slice(0, 1), slice(1, 2)),) * 3
+
+    def b_pass_one(j, k, which):
+        dev, pos = ring(j)
+        first = jnp.where(y_first(j), lax.rem(j, 2), 1 - yl)
+        index = first if which == 0 else 1 - first
+        place, far = jnp.where(index == 0, 3, 1), jnp.where(index == 0, 1, 3)
+        ref = tile.at[j, pos(order[k], place)]
+        wait(ref, b_sem.at[index, j, k])
+        if PARTS[k][which] is not None:
+            ref = ref.at[PARTS[k][which]]
+            send(ref, ref, b_send.at[j], b_fwd.at[which, j, k], dev(0, far))
+
+    def b_pass_half(j, which):
+        for k in range(4):
+            b_pass_one(j, k, which)
+
+    def input_grad(j):
+        lhs = [tile[j, pl.ds(d * 8, 8), 1, i].reshape(TOK, 128) for i in range(SUB)]
+        ig_acc[...] += dot(jnp.concatenate(lhs, axis=1) if SUB > 1 else lhs[0], win[j], 1, 1)
+
     def b_pass(j):
-        dev, pos = ring(j)
-        for k, da in enumerate(order):
-            ref = tile.at[j, pos(da, 3)]
-            wait(ref, b_sem.at[0, j, k])
-            send(ref.at[0], ref.at[0], b_send.at[j], b_fwd.at[0, j, k], dev(0, 1))
-            ref = tile.at[j, pos(da, 1)]
-            wait(ref, b_sem.at[1, j, k])
-            send(ref.at[1], ref.at[1], b_send.at[j], b_fwd.at[1, j, k], dev(0, 3))
+        for k in range(4):
+            b_pass_one(j, k, 0)
+            b_pass_one(j, k, 1)
+
+        @pl.when(jnp.logical_not(y_first(j)))
+        def _():
+            input_grad(j)
 
     def weight_grads(j):
         dev, pos = ring(j)
         for k, da in enumerate(order):
             ref = tile.at[j, pos(da, 2)]
-            wait(ref.at[0], b_fwd.at[0, j, k])
-            wait(ref.at[1], b_fwd.at[1, j, k])
+            for which in range(2):
+                if PARTS[k][which] is not None:
+                    wait(ref.at[PARTS[k][which]], b_fwd.at[which, j, k])
         for i in range(SUB):
             act = jnp.concatenate([tile[j, p, 0, i] for p in range(16)], axis=1)
             s_out[pl.ds(pl.multiple_of(j * W + i * 128, 128), 128), :] = dot(act, gc[...]).astype(BF)
@@ -222,6 +244,13 @@
         pltpu.make_async_copy(s_out.at[rows(j), mine], to, o_own.at[1, j]).start()
         send(s_out.at[rows(j), theirs], to, o_send.at[1, j], o_core.at[1, j], core)
 
+    def weight_and_input_grads(j):
+        weight_grads(j)
+
+        @pl.when(y_first(j))
+        def _():
+            input_grad(j)
+
     def piece(of, z):
         tok = pl.ds(pl.multiple_of(of * TOK + z * 128, 128), 128)
         return xt.at[mine, tok], gc.at[tok, mine]
@@ -250,15 +279,17 @@
         wait(xt.at[theirs, other_tok], xo_sem.at[1])
         wait(gc.at[other_tok, theirs], xo_sem.at[2])
 
-    def stage(t, lag, run):
-        @pl.when((t >= lag) & (t < NC + lag))
+    def stage(t, lag, run, last=LAST):
+        @pl.when((t >= lag) & (t <= last + lag))
         def _():
             run(t - lag)
 
     def at(t, when, run):
         pl.when(t == when)(run)
 
-    @pl.loop(0, NC + L7)
+    ig_acc[...] = jnp.zeros_like(ig_acc)
+
+    @pl.loop(0, LAST + L6)
     def _(t):
         stage(t, L1, add_and_pass)
         stage(t, L2, to_pair)
@@ -270,24 +301,26 @@
         at(t, L7, await_inputs)
         stage(t, L4, a_pass)
         stage(t, L5, a_last)
-        stage(t, L6, b_pass)
-        stage(t, L7, weight_grads)
-
-    total = None
-    for j in range(NC):
-        lhs = [tile[j, pl.ds(d * 8, 8), 1, i].reshape(TOK, 128) for i in range(SUB)]
-        term = dot(jnp.concatenate(lhs, axis=1) if SUB > 1 else lhs[0], win[j], 1, 1)
-        total = term if total is None else total + term
-    total = total.astype(BF)
-    ig_buf[0] = jnp.where(c == 0, total[:, :DC], total[:, DC:])
-    ig_buf[1] = jnp.where(c == 0, total[:, DC:], total[:, :DC])
+        stage(t, L6, b_pass, LAST - 1)
+        stage(t, L7, weight_and_input_grads, LAST - 2)
+
+    b_pass_half(LAST, 0)
+    input_grad(LAST)
+    keep = ig_acc[:, mine].astype(BF)
+    ig_buf[1] = ig_acc[:, theirs].astype(BF)
     send(ig_buf.at[1], ig_core, ic_send.at[0], ic_sem.at[0], core)
+    b_pass_half(LAST, 1)
     wait(ig_core, ic_sem.at[0])
-    ig_buf[0] = (ig_buf[0].astype(F32) + ig_core[...].astype(F32)).astype(BF)
+    ig_buf[0] = (keep.astype(F32) + ig_core[...].astype(F32)).astype(BF)
     for k in range(7):
         to_z = lax.rem(s + k + 1, 8)
         tok = pl.ds(pl.multiple_of(to_z * 128, 128), 128)
         send(ig_buf.at[0, tok], ig_z.at[k], iz_send.at[k], iz_sem.at[k], peers[k])
+
+    @pl.loop(LAST - 1, NC)
+    def _(j):
+        weight_grads(j)
+
     result = ig_buf[0, pl.ds(pl.multiple_of(s * 128, 128), 128), :].astype(F32)
     for k in range(7):
         wait(ig_z.at[k], iz_sem.at[k])
@@ -323,19 +356,27 @@
         wait(gwout_out.at[hidden(1 - c, j)], o_core.at[1, j])
 
 
+def write_out(a_ref, b_ref, c_ref, a_out, b_out, c_out, sem):
+    copies = [
+        pltpu.make_async_copy(src, dst, sem.at[i])
+        for i, (src, dst) in enumerate(((b_ref, b_out), (c_ref, c_out), (a_ref, a_out)))
+    ]
+    for copy in copies:
+        copy.start()
+    for copy in copies:
+        copy.wait()
+
+
 def local(normed_input, out_grad, w_in, w_out):
     any_space = pl.BlockSpec(memory_space=pl.ANY)
     dma = lambda *shape: pltpu.SemaphoreType.DMA(shape)
     vm = lambda *shape: pltpu.VMEM(shape, BF)
-    return pl.pallas_call(
+    shapes = [(128, DC), (DC, 2 * FH), (2 * FH, DC)]
+    grads = pl.pallas_call(
         kernel,
-        out_shape=[
-            jax.ShapeDtypeStruct((128, DC), BF),
-            jax.ShapeDtypeStruct((DC, 2 * FH), BF),
-            jax.ShapeDtypeStruct((2 * FH, DC), BF),
-        ],
+        out_shape=[vm(*shape) for shape in shapes],
         in_specs=[any_space] * 4,
-        out_specs=[pl.BlockSpec(memory_space=pltpu.VMEM), any_space, any_space],
+        out_specs=[pl.BlockSpec(memory_space=pltpu.VMEM)] * 3,
         scratch_shapes=[
             vm(TOK, 2 * DC),
             vm(2 * DC, 2 * TOK),
@@ -352,6 +393,7 @@
             vm(NC, 16, 2, SUB, 128, 128),
             vm(NC, 2 * DC, W),
             vm(FH, 2 * DC),
+            pltpu.VMEM((TOK, 2 * DC), F32),
             vm(2, TOK, DC),
             vm(TOK, DC),
             vm(7, 128, DC),
@@ -365,10 +407,17 @@
             dma(1), dma(1), dma(7), dma(7),
         ],
         compiler_params=pltpu.CompilerParams(
-            collective_id=0, has_side_effects=True, vmem_limit_bytes=62 << 20
+            collective_id=0, has_side_effects=True, vmem_limit_bytes=56 << 20
         ),
         cost_estimate=pl.CostEstimate(flops=17 * 10**9, bytes_accessed=12 * 10**6, transcendentals=0),
     )(normed_input, out_grad, w_in, w_out)
+    return pl.pallas_call(
+        write_out,
+        out_shape=[jax.ShapeDtypeStruct(shape, BF) for shape in shapes],
+        in_specs=[pl.BlockSpec(memory_space=pltpu.VMEM)] * 3,
+        out_specs=[any_space] * 3,
+        scratch_shapes=[dma(3)],
+    )(*grads)
 
 
 def solution(mesh):

time: 180 us -> 156 us (0.87)
  Pallas kernels: 173 us -> 152 us
  local copies, waits for them, and re-layouts: 6.32 us -> 3.46 us
    pallas_call x1 -> x2, Pallas kernels: 173 us -> 152 us  [the longest x1 147 us: local(): pl.pallas_call(kernel, out_shape=[vm(*shape) for shape in shapes], in_spe...]
    unnamed x5 -> x6, local copies, waits for them, and re-layouts: 6.32 us -> 3.46 us
where the time goes in v2:
time: 156 us
  Pallas kernels  152 us (97%)
  local copies, waits for them, and re-layouts  3.46 us (2%)
    pallas_call x1, Pallas kernels, local(): pl.pallas_call(kernel, out_shape=[vm(*shape) for shape in shapes], in_spe...  147 us
    pallas_call x1, Pallas kernels, local(): pl.pallas_call(write_out, out_shape=[jax.ShapeDtypeStruct(shape, BF) for...  4.62 us
    unnamed x6, local copies, waits for them, and re-layouts  3.46 us

profile of v2, /device:TPU:1, one launch (start us, length us, event | category | flops | bytes accessed | tf_op | source)
XLA Modules:
  0.0 155.8 jit_solution(11825292715281464625)
XLA Ops:
  0.6 147.1 %shard_map.67 = (bf16[128,384]{1,0:T(8,128)(2,1)S(1)}, bf16[384,3072]{1,0:T(8,128)(2,1)S(1)}, bf16[3072,384]{1,0:T(8,128)(2,1)S(1)}) custom-call(bf16[1024,384]{1,0:T(8,128)(2,1)} %x_in.1, bf16[1024,384]{1,0:T(8,128)(2,1)} %g_in.1, bf16[384,3072]{1,0:T(8,128)(2,1)} %win_in.1, bf16[3072,384]{1,0:T(8,128)(2,1)} %wout_in.1), custom_call_target="tpu_custom_call" | custom-call | flops 16999999488 | bytes 12000000 | tf_op jit(solution)/shard_map/pallas_call | solution.py:375
  147.7 0.0 copy-start
  147.7 1.4 copy-done
  149.1 0.0 copy-start.1
  149.1 1.4 copy-done.1
  150.5 0.0 copy-start.2
  150.5 0.6 copy-done.2
  151.2 4.6 %shard_map.68 = (bf16[128,384]{1,0:T(8,128)(2,1)}, bf16[384,3072]{1,0:T(8,128)(2,1)}, bf16[3072,384]{1,0:T(8,128)(2,1)}) custom-call(bf16[128,384]{1,0:T(8,128)(2,1)} %copy-done.2, bf16[384,3072]{1,0:T(8,128)(2,1)} %copy-done, bf16[3072,384]{1,0:T(8,128)(2,1)} %copy-done.1), custom_call_target="tpu_custom_call" | custom-call | tf_op jit(solution)/shard_map/pallas_call | solution.py:414
Async XLA Ops:
  147.7 1.4 copy-start
  149.1 1.4 copy-start.1
  150.5 0.6 copy-start.2

commit v3 on v2

--- a/solution.py
+++ b/solution.py
@@ -94,30 +94,43 @@
     barrier = pltpu.get_barrier_semaphore()
     for peer in everyone:
         pl.semaphore_signal(barrier, inc=1, device_id=peer, device_id_type=MESH)
+    ig_acc[...] = jnp.zeros_like(ig_acc)
     pl.semaphore_wait(barrier, len(everyone))
 
+    def swap_w_in(j):
+        send(win_in.at[:, hidden(1 - c, j)], win.at[j, mine], w_send.at[0, j], w_core.at[0, j], core)
+
+    def swap_w_out(j):
+        send(wout_in.at[hidden(1 - c, j)], wout.at[rows(j), mine], w_send.at[1, j], w_core.at[1, j], core)
+
     send(x_in, xc.at[:, mine], core_send.at[0], core_sem.at[0], core)
+    swap_w_in(0)
     send(g_in, gc.at[own_tok, mine], core_send.at[1], core_sem.at[1], core)
-
-    @pl.loop(0, NC)
+    swap_w_out(0)
+
+    @pl.loop(1, NC)
     def _(j):
-        send(win_in.at[:, hidden(1 - c, j)], win.at[j, mine], w_send.at[0, j], w_core.at[0, j], core)
-        send(wout_in.at[hidden(1 - c, j)], wout.at[rows(j), mine], w_send.at[1, j], w_core.at[1, j], core)
+        swap_w_in(j)
+        swap_w_out(j)
 
     wait(xc.at[:, mine], load_sem.at[0])
-    wait(gc.at[own_tok, mine], load_sem.at[1])
     wait(xc.at[:, theirs], core_sem.at[0])
-    wait(gc.at[own_tok, theirs], core_sem.at[1])
 
     nxt, prv, opp = lax.rem(x + 1, 4), lax.rem(x + 3, 4), lax.rem(x + 2, 4)
 
     def partial_sums(j):
         wait(win.at[j, mine], w_load.at[0, j])
-        wait(wout.at[rows(j), mine], w_load.at[1, j])
         wait(win.at[j, theirs], w_core.at[0, j])
-        wait(wout.at[rows(j), theirs], w_core.at[1, j])
         pre = dot(xc[...], win[j]).astype(BF)
         part[j, :, 0] = pre.reshape(8, 128, W)
+
+        @pl.when(j == 0)
+        def _():
+            wait(gc.at[own_tok, mine], load_sem.at[1])
+            wait(gc.at[own_tok, theirs], core_sem.at[1])
+
+        wait(wout.at[rows(j), mine], w_load.at[1, j])
+        wait(wout.at[rows(j), theirs], w_core.at[1, j])
         grad = dot(gc[own_tok, :], wout[rows(j), :], 1, 1).astype(BF)
         part[j, :, 1] = grad.reshape(8, 128, W)
         send(part.at[j, opp * 2], r_opp.at[j, 0], rs_send.at[0, j], rs_sem.at[0, j], right)
@@ -144,14 +157,23 @@
         y_buf[j] = x_sum(j, 1 - yl).astype(BF)
         send(y_buf.at[j], r_y.at[j], y_send.at[j], y_sem.at[j], pair)
 
+    up, down = device(x, y + 1, s, c), device(x, y + 3, s, c)
+    x_part = [lax.rem(x + i, 4) * 2 for i in range(4)]
+    y_part = [(lax.rem(y + i, 4) // 2) * 8 + lax.rem(y + i, 2) for i in range(4)]
+
+    def choose(yf, a, b):
+        return tuple(jnp.where(yf, p, q) for p, q in zip(a, b))
+
     def ring(j):
         yf = y_first(j)
+        ahead = {"a": choose(yf, up, right), "b": choose(yf, right, up)}
+        behind = {"a": choose(yf, down, left), "b": choose(yf, left, down)}
 
         def dev(da, db):
-            return device(jnp.where(yf, x + db, x + da), jnp.where(yf, y + da, y + db), s, c)
+            return (ahead if da + db == 1 else behind)["a" if da else "b"]
 
         def pos(da, db):
-            return position(jnp.where(yf, x + db, x + da), jnp.where(yf, y + da, y + db))
+            return jnp.where(yf, x_part[db] + y_part[da], x_part[da] + y_part[db])
 
         return dev, pos
 
@@ -198,15 +220,18 @@
     PARTS = ((slice(0, 2), None),) + ((slice(0, 1), slice(1, 2)),) * 3
 
     def b_pass_one(j, k, which):
-        dev, pos = ring(j)
-        first = jnp.where(y_first(j), lax.rem(j, 2), 1 - yl)
-        index = first if which == 0 else 1 - first
-        place, far = jnp.where(index == 0, 3, 1), jnp.where(index == 0, 1, 3)
-        ref = tile.at[j, pos(order[k], place)]
+        yf = y_first(j)
+        index = jnp.where(yf, lax.rem(j, 2), 1 - yl)
+        index = index if which == 0 else 1 - index
+        back = index == 0
+        da = order[k]
+        near = [jnp.where(yf, x_part[db] + y_part[da], x_part[da] + y_part[db]) for db in (3, 1)]
+        ref = tile.at[j, jnp.where(back, near[0], near[1])]
         wait(ref, b_sem.at[index, j, k])
         if PARTS[k][which] is not None:
             ref = ref.at[PARTS[k][which]]
-            send(ref, ref, b_send.at[j], b_fwd.at[which, j, k], dev(0, far))
+            to = choose(back, choose(yf, right, up), choose(yf, left, down))
+            send(ref, ref, b_send.at[j], b_fwd.at[which, j, k], to)
 
     def b_pass_half(j, which):
         for k in range(4):
@@ -287,44 +312,53 @@
     def at(t, when, run):
         pl.when(t == when)(run)
 
-    ig_acc[...] = jnp.zeros_like(ig_acc)
-
     @pl.loop(0, LAST + L6)
     def _(t):
+        stage(t, L4, a_pass)
+        stage(t, L3, activation)
+        stage(t, L5, a_last)
+        stage(t, L2, to_pair)
         stage(t, L1, add_and_pass)
-        stage(t, L2, to_pair)
-        stage(t, L3, activation)
         stage(t, 0, partial_sums)
         at(t, 0, turn_inputs)
-        at(t, 2, spread_inputs)
+        at(t, 1, spread_inputs)
         at(t, L7 - 1, finish_inputs)
         at(t, L7, await_inputs)
-        stage(t, L4, a_pass)
-        stage(t, L5, a_last)
         stage(t, L6, b_pass, LAST - 1)
-        stage(t, L7, weight_and_input_grads, LAST - 2)
+        stage(t, L7, weight_and_input_grads, LAST + L6 - 1 - L7)
+
+    def z_step(n):
+        for way, to in enumerate((peers[0], peers[6])):
+            start = lax.rem(s + (4 - n if way == 0 else 4 + n), 8) * 128
+            half = pl.ds(pl.multiple_of(start + way * 64, 64), 64)
+            block = pl.ds(pl.multiple_of(start, 128), 128)
+            if n == 0:
+                send(ig_buf.at[0, half], ig_z.at[way, 0, pl.ds(0, 64)], iz_send.at[way, 0], iz_sem.at[way, 0], to)
+                continue
+            came = ig_z.at[way, 0, pl.ds(0, 64)] if n == 1 else ig_z.at[way, n - 1]
+            rows_in = half if n == 1 else block
+            wait(came, iz_sem.at[way, n - 1])
+            ig_buf[0, rows_in] = (ig_buf[0, rows_in].astype(F32) + came[...].astype(F32)).astype(BF)
+            send(ig_buf.at[0, block], ig_z.at[way, n], iz_send.at[way, n], iz_sem.at[way, n], to)
 
     b_pass_half(LAST, 0)
     input_grad(LAST)
     keep = ig_acc[:, mine].astype(BF)
     ig_buf[1] = ig_acc[:, theirs].astype(BF)
     send(ig_buf.at[1], ig_core, ic_send.at[0], ic_sem.at[0], core)
-    b_pass_half(LAST, 1)
     wait(ig_core, ic_sem.at[0])
     ig_buf[0] = (keep.astype(F32) + ig_core[...].astype(F32)).astype(BF)
-    for k in range(7):
-        to_z = lax.rem(s + k + 1, 8)
-        tok = pl.ds(pl.multiple_of(to_z * 128, 128), 128)
-        send(ig_buf.at[0, tok], ig_z.at[k], iz_send.at[k], iz_sem.at[k], peers[k])
-
-    @pl.loop(LAST - 1, NC)
-    def _(j):
-        weight_grads(j)
-
+    z_step(0)
+    b_pass_half(LAST, 1)
+    z_step(1)
+    weight_grads(LAST - 1)
+    z_step(2)
+    z_step(3)
+    weight_grads(LAST)
     result = ig_buf[0, pl.ds(pl.multiple_of(s * 128, 128), 128), :].astype(F32)
-    for k in range(7):
-        wait(ig_z.at[k], iz_sem.at[k])
-        result += ig_z[k].astype(F32)
+    for way in range(2):
+        wait(ig_z.at[way, 3], iz_sem.at[way, 3])
+        result += ig_z[way, 3].astype(F32)
     ig_out[...] = result.astype(BF)
 
     for i in range(2):
@@ -336,8 +370,10 @@
     wait(xt.at[mine, other_tok], xo_send.at[1])
     wait(gc.at[other_tok, mine], xo_send.at[2])
     wait(ig_buf.at[1], ic_send.at[0])
-    for k in range(7):
-        wait(ig_z.at[k], iz_send.at[k])
+    for way in range(2):
+        wait(ig_z.at[way, 0, pl.ds(0, 64)], iz_send.at[way, 0])
+        for n in range(1, 4):
+            wait(ig_z.at[way, n], iz_send.at[way, n])
 
     @pl.loop(0, NC)
     def _(j):
@@ -396,7 +432,7 @@
             pltpu.VMEM((TOK, 2 * DC), F32),
             vm(2, TOK, DC),
             vm(TOK, DC),
-            vm(7, 128, DC),
+            vm(2, 4, 128, DC),
             dma(2), dma(2), dma(2),
             dma(2, NC), dma(2, NC), dma(2, NC),
             dma(6, NC), dma(6, NC), dma(NC), dma(NC),
@@ -404,7 +440,7 @@
             dma(2, NC, 4), dma(2, NC, 4), dma(NC),
             dma(2), dma(2), dma(2, 7), dma(2, 7), dma(3), dma(3),
             dma(2, NC), dma(2, NC), dma(2, NC),
-            dma(1), dma(1), dma(7), dma(7),
+            dma(1), dma(1), dma(2, 4), dma(2, 4),
         ],
         compiler_params=pltpu.CompilerParams(
             collective_id=0, has_side_effects=True, vmem_limit_bytes=56 << 20

time: 156 us -> 152 us (0.974)
  Pallas kernels: 152 us -> 148 us
    pallas_call x1, Pallas kernels: 147 us -> 143 us  [local(): pl.pallas_call(kernel, out_shape=[vm(*shape) for shape in shapes], in_spe...]
where the time goes in v3:
time: 152 us
  Pallas kernels  148 us (97%)
  local copies, waits for them, and re-layouts  3.46 us (2%)
    pallas_call x1, Pallas kernels, local(): pl.pallas_call(kernel, out_shape=[vm(*shape) for shape in shapes], in_spe...  143 us
    pallas_call x1, Pallas kernels, local(): pl.pallas_call(write_out, out_shape=[jax.ShapeDtypeStruct(shape, BF) for...  4.62 us
    unnamed x6, local copies, waits for them, and re-layouts  3.46 us

profile of v3, /device:TPU:1, one launch (start us, length us, event | category | flops | bytes accessed | tf_op | source)
XLA Modules:
  0.0 151.8 jit_solution(14665777099005600223)
XLA Ops:
  0.6 143.1 %shard_map.67 = (bf16[128,384]{1,0:T(8,128)(2,1)S(1)}, bf16[384,3072]{1,0:T(8,128)(2,1)S(1)}, bf16[3072,384]{1,0:T(8,128)(2,1)S(1)}) custom-call(bf16[1024,384]{1,0:T(8,128)(2,1)} %x_in.1, bf16[1024,384]{1,0:T(8,128)(2,1)} %g_in.1, bf16[384,3072]{1,0:T(8,128)(2,1)} %win_in.1, bf16[3072,384]{1,0:T(8,128)(2,1)} %wout_in.1), custom_call_target="tpu_custom_call" | custom-call | flops 16999999488 | bytes 12000000 | tf_op jit(solution)/shard_map/pallas_call | solution.py:411
  143.7 0.0 copy-start
  143.7 1.4 copy-done
  145.1 0.0 copy-start.1
  145.1 1.4 copy-done.1
  146.5 0.0 copy-start.2
  146.5 0.6 copy-done.2
  147.2 4.6 %shard_map.68 = (bf16[128,384]{1,0:T(8,128)(2,1)}, bf16[384,3072]{1,0:T(8,128)(2,1)}, bf16[3072,384]{1,0:T(8,128)(2,1)}) custom-call(bf16[128,384]{1,0:T(8,128)(2,1)} %copy-done.2, bf16[384,3072]{1,0:T(8,128)(2,1)} %copy-done, bf16[3072,384]{1,0:T(8,128)(2,1)} %copy-done.1), custom_call_target="tpu_custom_call" | custom-call | tf_op jit(solution)/shard_map/pallas_call | solution.py:450
Async XLA Ops:
  143.7 1.4 copy-start
  145.1 1.4 copy-start.1
  146.5 0.6 copy-start.2

commit v4 on v3

--- a/solution.py
+++ b/solution.py
@@ -260,14 +260,14 @@
         for i in range(SUB):
             act = jnp.concatenate([tile[j, p, 0, i] for p in range(16)], axis=1)
             s_out[pl.ds(pl.multiple_of(j * W + i * 128, 128), 128), :] = dot(act, gc[...]).astype(BF)
+        to = gwout_out.at[hidden(c, j)]
+        pltpu.make_async_copy(s_out.at[rows(j), mine], to, o_own.at[1, j]).start()
+        send(s_out.at[rows(j), theirs], to, o_send.at[1, j], o_core.at[1, j], core)
         grads = [tile[j, :, 1, i].reshape(2 * TOK, 128) for i in range(SUB)]
         s_in[j] = dot(xt[...], jnp.concatenate(grads, axis=1) if SUB > 1 else grads[0]).astype(BF)
         to = gwin_out.at[:, hidden(c, j)]
         pltpu.make_async_copy(s_in.at[j, mine], to, o_own.at[0, j]).start()
         send(s_in.at[j, theirs], to, o_send.at[0, j], o_core.at[0, j], core)
-        to = gwout_out.at[hidden(c, j)]
-        pltpu.make_async_copy(s_out.at[rows(j), mine], to, o_own.at[1, j]).start()
-        send(s_out.at[rows(j), theirs], to, o_send.at[1, j], o_core.at[1, j], core)
 
     def weight_and_input_grads(j):
         weight_grads(j)

time: 152 us -> 153 us (level)
  no operation moved by 1% of the time
where the time goes in v4:
time: 153 us
  Pallas kernels  149 us (97%)
  local copies, waits for them, and re-layouts  3.46 us (2%)
    pallas_call x1, Pallas kernels, local(): pl.pallas_call(kernel, out_shape=[vm(*shape) for shape in shapes], in_spe...  144 us
    pallas_call x1, Pallas kernels, local(): pl.pallas_call(write_out, out_shape=[jax.ShapeDtypeStruct(shape, BF) for...  4.62 us
    unnamed x6, local copies, waits for them, and re-layouts  3.46 us

profile of v4, /device:TPU:1, one launch (start us, length us, event | category | flops | bytes accessed | tf_op | source)
XLA Modules:
  0.0 153.1 jit_solution(11188433065976688211)
XLA Ops:
  0.6 144.3 %shard_map.67 = (bf16[128,384]{1,0:T(8,128)(2,1)S(1)}, bf16[384,3072]{1,0:T(8,128)(2,1)S(1)}, bf16[3072,384]{1,0:T(8,128)(2,1)S(1)}) custom-call(bf16[1024,384]{1,0:T(8,128)(2,1)} %x_in.1, bf16[1024,384]{1,0:T(8,128)(2,1)} %g_in.1, bf16[384,3072]{1,0:T(8,128)(2,1)} %win_in.1, bf16[3072,384]{1,0:T(8,128)(2,1)} %wout_in.1), custom_call_target="tpu_custom_call" | custom-call | flops 16999999488 | bytes 12000000 | tf_op jit(solution)/shard_map/pallas_call | solution.py:411
  145.0 0.0 copy-start
  145.0 1.4 copy-done
  146.4 0.0 copy-start.1
  146.4 1.4 copy-done.1
  147.8 0.0 copy-start.2
  147.8 0.6 copy-done.2
  148.4 4.6 %shard_map.68 = (bf16[128,384]{1,0:T(8,128)(2,1)}, bf16[384,3072]{1,0:T(8,128)(2,1)}, bf16[3072,384]{1,0:T(8,128)(2,1)}) custom-call(bf16[128,384]{1,0:T(8,128)(2,1)} %copy-done.2, bf16[384,3072]{1,0:T(8,128)(2,1)} %copy-done, bf16[3072,384]{1,0:T(8,128)(2,1)} %copy-done.1), custom_call_target="tpu_custom_call" | custom-call | tf_op jit(solution)/shard_map/pallas_call | solution.py:450
Async XLA Ops:
  145.0 1.4 copy-start
  146.4 1.4 copy-start.1
  147.8 0.6 copy-start.2
